TPU v7x, 256 devices: a whole 4x4x8 slice. The times are simulated.
256 devices in a mesh: seq: 64 (over y_hi, x, z), dp: 4 (over y_lo, core).
Axes of the slice: x: 4, y: 4 (y_hi: 2, y_lo: 2; y = y_hi * 2 + y_lo), z: 8, core: 2. Of those that a mesh axis runs over, the one named last changes fastest.
Arguments:
- signal: bfloat16 [4, 32768, 256], P('dp', 'seq'), may hold values from -6 to 6
- cotangent: bfloat16 [4, 32768, 256], P('dp', 'seq'), may hold values from -6 to 6
- filter_codes: bfloat16 [32768, 256], P('seq'), may hold values from -0.03125 to 0.03125
- keep_mask: int32 [32768, 256], P('seq'), may hold values 0 or 1
- exponents: int32 [256], replicated, may hold values from -2 to 2
- skip: float32 [256], replicated, may hold values from -1 to 1
Outputs:
- input_grad: bfloat16 [4, 32768, 256], P('dp', 'seq')
- filter_grad: float32 [32768, 256], P('seq')
All inputs are finite; a program needn't handle non-finite values. No bound on the sum of `keep_mask` on one device may be relied on, other than what follows from the above.
Results may differ from a plain program's by a relative error of at most 0.014.
Values may be sent and summed in bfloat16 or wider, within the bound.
A program may use at most 64 MiB of HBM per device.

v0:
```python
import functools
import math

import jax
import jax.numpy as jnp
import numpy as np
from jax import lax
from jax.experimental import pallas as pl
from jax.experimental.pallas import tpu as pltpu
from jax.sharding import PartitionSpec as P

MESH = pl.DeviceIdType.MESH
F32 = jnp.float32
BF16 = jnp.bfloat16
LANES = 128
ROWS = 4
SEQ = 64
DP = 4
ALL = SEQ * DP
HALF = SEQ * ROWS
POINTS = 2 * HALF * LANES
VMEM_LIMIT = 48 << 20


def split(values):
    high = values.astype(BF16)
    return high, (values - high.astype(F32)).astype(BF16)


def np_split(values):
    values = values.astype(np.float32)
    high = values.astype(jnp.bfloat16)
    return high, (values - high.astype(np.float32)).astype(jnp.bfloat16)


def tables():
    rows = (ROWS * np.arange(SEQ)[None, :] + np.arange(ROWS)[:, None]).reshape(-1)
    odd = 2 * np.arange(HALF) + 1
    angle = 2 * np.pi / (4 * HALF) * ((odd[:, None] * rows[None, :]) % (4 * HALF))
    first = np.concatenate([np.cos(angle), -np.sin(angle)], axis=0)
    lane = np.arange(LANES)
    angle = 2 * np.pi / (2 * POINTS) * ((odd[:, None] * lane[None, :]) % (2 * POINTS))
    turn = np.concatenate([np.cos(angle), -np.sin(angle)], axis=1).astype(np.float32)
    angle = 2 * np.pi / LANES * ((lane[:, None] * lane[None, :]) % LANES)
    cos, sin = np.cos(angle), np.sin(angle)
    second = np.block([[cos, -sin], [sin, cos]])
    first_high, first_low = np_split(first)
    second_high, second_low = np_split(second)
    return (
        np.concatenate([first_high, first_low], axis=1),
        turn,
        np.concatenate([second_high, second_high, second_low], axis=0),
        np.concatenate([second_high.T, second_high.T, second_low.T], axis=0),
        np.concatenate([first_high.T, first_low.T, first_high.T], axis=1),
    )


def dot(left, right):
    return jnp.dot(left, right, preferred_element_type=F32)


def dot_nt(left, right):
    return lax.dot_general(left, right, (((1,), (1,)), ((), ())), preferred_element_type=F32)


def same(shape, offset=0, factor=1):
    row = lax.broadcasted_iota(jnp.int32, shape, 0)
    column = lax.broadcasted_iota(jnp.int32, shape, 1)
    return jnp.where(column == factor * row + offset, 1.0, 0.0).astype(BF16)


def mix(values, matrix):
    high, low = split(values)
    return dot(jnp.concatenate([high, low, high], axis=1), matrix)


def forward(rows, first, turn, second):
    both = dot(first, jnp.concatenate([rows, rows], axis=0))
    real, imag = both[:HALF], both[HALF:]
    cos, sin = turn[:, :LANES], turn[:, LANES:]
    turned = jnp.concatenate([real * cos - imag * sin, real * sin + imag * cos], axis=1)
    return mix(turned, second)


def backward(spectrum, turn, second_back, first_back):
    both = mix(spectrum, second_back)
    real, imag = both[:, :LANES], both[:, LANES:]
    cos, sin = turn[:, :LANES], turn[:, LANES:]
    turned = jnp.concatenate([real * cos + imag * sin, imag * cos - real * sin], axis=0)
    high, low = split(turned)
    return dot(first_back, jnp.concatenate([high, high, low], axis=0))


def conj_product(left, right):
    left_real, left_imag = left[:, :LANES], left[:, LANES:]
    right_real, right_imag = right[:, :LANES], right[:, LANES:]
    return jnp.concatenate(
        [
            left_real * right_real + left_imag * right_imag,
            left_real * right_imag - left_imag * right_real,
        ],
        axis=1,
    )


def main_kernel(
    signal, cotangent, codes, exponents, skip, first, turn, second, second_back, first_back,
    home,
    wide, wide_codes, out_buf, codes_buf, in_buf, codes_in, back_buf, spec_g, spec_h,
    send_sem, recv_sem,
):
    s, d = lax.axis_index("seq"), lax.axis_index("dp")
    me = s * DP + d
    place = d * SEQ + s

    barrier = pltpu.get_barrier_semaphore()

    def greet(step, carry):
        other = lax.rem(me + step, ALL)
        pl.semaphore_signal(
            barrier, inc=1, device_id=(other // DP, lax.rem(other, DP)), device_id_type=MESH
        )
        return carry

    lax.fori_loop(1, ALL, greet, 0, unroll=15)

    eye = same((ALL, ALL))
    for base, array in ((0, signal), (ROWS, cotangent)):
        turned = dot_nt(eye, array[...])
        for row in range(ROWS):
            wide[pl.ds(base + row, ALL, 2 * ROWS), :] = turned[:, row * LANES : (row + 1) * LANES]
    out_buf[...] = wide[...].reshape(ALL, 2 * ROWS, LANES).astype(BF16)
    turned = dot_nt(same((SEQ, ALL), d, DP), codes[...])
    wide_codes[...] = jnp.zeros_like(wide_codes)
    for row in range(ROWS):
        wide_codes[pl.ds(row, SEQ, 2 * ROWS), :] = turned[:, row * LANES : (row + 1) * LANES]
    codes_buf[...] = wide_codes[...].reshape(SEQ, 2 * ROWS, LANES).astype(BF16)

    pl.semaphore_wait(barrier, ALL - 1)

    def send_codes(step, carry):
        other = lax.rem(s + step, SEQ)
        pltpu.make_async_remote_copy(
            src_ref=codes_buf.at[other], dst_ref=codes_in.at[s],
            send_sem=send_sem.at[0], recv_sem=recv_sem.at[0],
            device_id=(other, d), device_id_type=MESH,
        ).start()
        return carry

    lax.fori_loop(1, SEQ, send_codes, 0, unroll=9)

    def send_rows(step, carry):
        other = lax.rem(me + step, ALL)
        pltpu.make_async_remote_copy(
            src_ref=out_buf.at[other], dst_ref=in_buf.at[place],
            send_sem=send_sem.at[1], recv_sem=recv_sem.at[1],
            device_id=(other // DP, lax.rem(other, DP)), device_id_type=MESH,
        ).start()
        return carry

    lax.fori_loop(1, ALL, send_rows, 0, unroll=15)
    codes_in[pl.ds(s, 1)] = codes_buf[pl.ds(s, 1)]
    in_buf[pl.ds(place, 1)] = out_buf[pl.ds(me, 1)]

    def drain(source, target, index, count):
        every = pltpu.make_async_remote_copy(
            src_ref=source.at[pl.ds(0, count)], dst_ref=target.at[pl.ds(0, count)],
            send_sem=send_sem.at[index], recv_sem=recv_sem.at[index],
            device_id=(s, d), device_id_type=MESH,
        )
        every.wait_recv()
        every.wait_send()

    drain(codes_buf, codes_in, 0, SEQ - 1)
    wide_codes[...] = codes_in[...].reshape(SEQ * 2 * ROWS, LANES).astype(F32)
    rows = jnp.concatenate(
        [wide_codes[pl.ds(row, SEQ, 2 * ROWS), :] for row in range(ROWS)], axis=0
    ).astype(BF16)
    spec_h[...] = forward(rows, first[...], turn[...], second[...])

    drain(out_buf, in_buf, 1, ALL - 1)
    wide[...] = in_buf[...].reshape(ALL * 2 * ROWS, LANES).astype(F32)

    unit = jnp.full((1, LANES), exponents[me].astype(F32), F32)
    scale = jnp.exp2(unit) * (2.0 / POINTS)
    direct = skip[me]

    def rows_of(index, base):
        start = index * (SEQ * 2 * ROWS) + base
        return jnp.concatenate(
            [wide[pl.ds(start + row, SEQ, 2 * ROWS), :] for row in range(ROWS)], axis=0
        )

    spec_g[...] = jnp.zeros_like(spec_g)
    for index in range(DP):
        start = index * (SEQ * 2 * ROWS)
        cot = rows_of(index, ROWS)
        cot_spec = forward(cot.astype(BF16), first[...], turn[...], second[...])
        sig_spec = forward(rows_of(index, 0).astype(BF16), first[...], turn[...], second[...])
        spec_g[...] += conj_product(sig_spec, cot_spec)
        back = backward(
            conj_product(spec_h[...], cot_spec), turn[...], second_back[...], first_back[...]
        )
        grad = back * scale + direct * cot
        for row in range(ROWS):
            wide[pl.ds(start + row, SEQ, 2 * ROWS), :] = grad[row * SEQ : (row + 1) * SEQ]
    total = backward(spec_g[...], turn[...], second_back[...], first_back[...]) * (2.0 / POINTS)
    for index in range(DP):
        start = index * (SEQ * 2 * ROWS) + ROWS
        for row in range(ROWS):
            wide[pl.ds(start + row, SEQ, 2 * ROWS), :] = total[row * SEQ : (row + 1) * SEQ]
    back_buf[...] = wide[...].reshape(ALL, 2 * ROWS, LANES).astype(BF16)

    def send_back(step, carry):
        other = lax.rem(me + step, ALL)
        to_seq, to_dp = other // DP, lax.rem(other, DP)
        pltpu.make_async_remote_copy(
            src_ref=back_buf.at[to_dp * SEQ + to_seq], dst_ref=home.at[me],
            send_sem=send_sem.at[2], recv_sem=recv_sem.at[2],
            device_id=(to_seq, to_dp), device_id_type=MESH,
        ).start()
        return carry

    lax.fori_loop(1, ALL, send_back, 0, unroll=15)
    home[pl.ds(me, 1)] = back_buf[pl.ds(place, 1)]
    drain(back_buf, home, 2, ALL - 1)


def last_kernel(home, mask, exponents, input_grad, filter_grad, wide):
    wide[...] = home[...].reshape(ALL * 2 * ROWS, LANES).astype(F32)
    eye = same((LANES, LANES))
    scale = jnp.exp2(exponents[...].astype(F32)) * (1.0 / math.sqrt(DP * HALF * LANES))
    for row in range(ROWS):
        part = pl.ds(row * LANES, LANES)
        grad = wide[pl.ds(row, ALL, 2 * ROWS), :].astype(BF16)
        input_grad[part, :] = dot_nt(eye, grad).astype(BF16)
        total = wide[pl.ds(ROWS + row, ALL, 2 * ROWS), :].astype(BF16)
        filter_grad[part, :] = mask[part, :].astype(F32) * scale * dot_nt(eye, total)


def per_device(signal, cotangent, filter_codes, keep_mask, exponents, skip):
    span, width = signal.shape[1], signal.shape[2]
    vmem = pl.BlockSpec(memory_space=pltpu.VMEM)
    smem = pl.BlockSpec(memory_space=pltpu.SMEM)
    home = pl.pallas_call(
        main_kernel,
        out_shape=jax.ShapeDtypeStruct((ALL, 2 * ROWS, LANES), BF16),
        in_specs=[vmem] * 3 + [smem] * 2 + [vmem] * 5,
        out_specs=vmem,
        scratch_shapes=[
            pltpu.VMEM((ALL * 2 * ROWS, LANES), F32),
            pltpu.VMEM((SEQ * 2 * ROWS, LANES), F32),
            pltpu.VMEM((ALL, 2 * ROWS, LANES), BF16),
            pltpu.VMEM((SEQ, 2 * ROWS, LANES), BF16),
            pltpu.VMEM((ALL, 2 * ROWS, LANES), BF16),
            pltpu.VMEM((SEQ, 2 * ROWS, LANES), BF16),
            pltpu.VMEM((ALL, 2 * ROWS, LANES), BF16),
            pltpu.VMEM((HALF, 2 * LANES), F32),
            pltpu.VMEM((HALF, 2 * LANES), F32),
            pltpu.SemaphoreType.DMA((3,)),
            pltpu.SemaphoreType.DMA((3,)),
        ],
        compiler_params=pltpu.CompilerParams(
            collective_id=0, has_side_effects=True, vmem_limit_bytes=VMEM_LIMIT
        ),
        name="main",
    )(
        signal.reshape(span, width), cotangent.reshape(span, width), filter_codes,
        exponents, skip, *[jnp.asarray(table) for table in tables()],
    )
    input_grad, filter_grad = pl.pallas_call(
        last_kernel,
        out_shape=(
            jax.ShapeDtypeStruct((span, width), BF16),
            jax.ShapeDtypeStruct((span, width), F32),
        ),
        in_specs=[vmem] * 3,
        out_specs=(vmem, vmem),
        scratch_shapes=[pltpu.VMEM((ALL * 2 * ROWS, LANES), F32)],
        compiler_params=pltpu.CompilerParams(vmem_limit_bytes=VMEM_LIMIT),
        name="last",
    )(home, keep_mask, exponents.reshape(1, width))
    return input_grad.reshape(signal.shape), filter_grad


def solution(mesh):
    return jax.shard_map(
        per_device,
        mesh=mesh,
        in_specs=(
            P("dp", "seq", None),
            P("dp", "seq", None),
            P("seq", None),
            P("seq", None),
            P(),
            P(),
        ),
        out_specs=(P("dp", "seq", None), P("seq", None)),
        check_vma=False,
    )
```

profile of v0, /device:TPU:1, one launch (start us, length us, event | category | flops | bytes accessed | tf_op | source)
XLA Modules:
  0.0 67.3 jit_solution(18419681593924765188)
XLA Ops:
  0.6 0.0 copy-start.10
  0.6 0.0 copy-start.9
  0.7 0.7 copy-done.10
  1.3 0.0 copy-done.9
  1.3 0.0 copy-start
  1.3 1.1 %copy-done = bf16[256,1536]{1,0:T(8,128)(2,1)S(1)} copy-done((bf16[256,1536]{1,0:T(8,128)(2,1)S(1)}, bf16[256,1536]{1,0:T(8,128)(2,1)}, u32[]{:S(2)}) %copy-start) | copy-done | bytes 786456
  2.5 0.0 copy-start.1
  2.5 1.0 %copy-done.1 = bf16[512,512]{1,0:T(8,128)(2,1)S(1)} copy-done((bf16[512,512]{1,0:T(8,128)(2,1)S(1)}, bf16[512,512]{1,0:T(8,128)(2,1)}, u32[]{:S(2)}) %copy-start.1) | copy-done | bytes 524312
  3.5 0.0 copy-start.3
  3.5 1.0 %copy-done.3 = bf16[768,256]{1,0:T(8,128)(2,1)S(1)} copy-done((bf16[768,256]{1,0:T(8,128)(2,1)S(1)}, bf16[768,256]{1,0:T(8,128)(2,1)}, u32[]{:S(2)}) %copy-start.3) | copy-done | bytes 393240
  4.5 0.0 copy-start.4
  4.5 1.0 %copy-done.4 = bf16[768,256]{1,0:T(8,128)(2,1)S(1)} copy-done((bf16[768,256]{1,0:T(8,128)(2,1)S(1)}, bf16[768,256]{1,0:T(8,128)(2,1)}, u32[]{:S(2)}) %copy-start.4) | copy-done | bytes 393240
  5.5 0.0 copy-start.5
  5.5 0.9 %copy-done.5 = bf16[1,512,256]{2,1,0:T(8,128)(2,1)S(1)} copy-done((bf16[1,512,256]{2,1,0:T(8,128)(2,1)S(1)}, bf16[1,512,256]{2,1,0:T(8,128)(2,1)}, u32[]{:S(2)}) %copy-start.5) | copy-done | bytes 262168
  6.4 0.0 copy-start.6
  6.4 0.9 %copy-done.6 = bf16[1,512,256]{2,1,0:T(8,128)(2,1)S(1)} copy-done((bf16[1,512,256]{2,1,0:T(8,128)(2,1)S(1)}, bf16[1,512,256]{2,1,0:T(8,128)(2,1)}, u32[]{:S(2)}) %copy-start.6) | copy-done | bytes 262168
  7.4 0.0 copy-start.7
  7.4 0.9 %copy-done.7 = bf16[512,256]{1,0:T(8,128)(2,1)S(1)} copy-done((bf16[512,256]{1,0:T(8,128)(2,1)S(1)}, bf16[512,256]{1,0:T(8,128)(2,1)}, u32[]{:S(2)}) %copy-start.7) | copy-done | bytes 262168
  8.3 0.0 copy-start.8
  8.3 0.9 %copy-done.8 = f32[256,256]{1,0:T(8,128)S(1)} copy-done((f32[256,256]{1,0:T(8,128)S(1)}, f32[256,256]{1,0:T(8,128)}, u32[]{:S(2)}) %copy-start.8) | copy-done | bytes 262168
  9.3 0.0 copy-start.2
  9.3 56.7 %main.1.home = bf16[256,8,128]{2,1,0:T(8,128)(2,1)S(1)} custom-call(bf16[512,256]{1,0:T(8,128)(2,1)S(1)} %bitcast.4, bf16[512,256]{1,0:T(8,128)(2,1)S(1)} %bitcast.5, bf16[512,256]{1,0:T(8,128)(2,1)S(1)} %copy-done.7, s32[256]{0:T(256)S(1)} %copy-done.9, f32[256]{0:T(256)S(1)} %copy-done.10, bf16[512,512]{1,0:T(8,128)(2,1)S(1)} %copy-done.1, ...), custom_call_target="tpu_custom_call" | custom-call | tf_op jit(solution)/shard_map/main/pallas_call | solution.py:245
  66.0 0.0 copy-done.2
  66.0 1.3 %last.1 = (bf16[512,256]{1,0:T(8,128)(2,1)}, f32[512,256]{1,0:T(8,128)}) custom-call(bf16[256,8,128]{2,1,0:T(8,128)(2,1)S(1)} %main.1.home, s32[512,256]{1,0:T(8,128)S(1)} %copy-done.2, s32[1,256]{1,0:T(1,128)S(1)} %bitcast.6), custom_call_target="tpu_custom_call" | custom-call | tf_op jit(solution)/shard_map/last/pallas_call | solution.py:271
Async XLA Ops:
  0.6 0.7 %copy-start.10 = (f32[256]{0:T(256)S(1)}, f32[256]{0:T(256)}, u32[]{:S(2)}) copy-start(f32[256]{0:T(256)} %skip.1) | copy-start | bytes 3076
  0.6 0.7 %copy-start.9 = (s32[256]{0:T(256)S(1)}, s32[256]{0:T(256)}, u32[]{:S(2)}) copy-start(s32[256]{0:T(256)} %exponents.1) | copy-start | bytes 3076
  1.3 1.1 %copy-start = (bf16[256,1536]{1,0:T(8,128)(2,1)S(1)}, bf16[256,1536]{1,0:T(8,128)(2,1)}, u32[]{:S(2)}) copy-start(bf16[256,1536]{1,0:T(8,128)(2,1)} %constant.14.clone.first_back) | copy-start | bytes 2359300
  2.5 1.0 %copy-start.1 = (bf16[512,512]{1,0:T(8,128)(2,1)S(1)}, bf16[512,512]{1,0:T(8,128)(2,1)}, u32[]{:S(2)}) copy-start(bf16[512,512]{1,0:T(8,128)(2,1)} %constant.10.clone.first) | copy-start | bytes 1572868
  3.5 1.0 %copy-start.3 = (bf16[768,256]{1,0:T(8,128)(2,1)S(1)}, bf16[768,256]{1,0:T(8,128)(2,1)}, u32[]{:S(2)}) copy-start(bf16[768,256]{1,0:T(8,128)(2,1)} %constant.13.clone.second_back) | copy-start | bytes 1179652
  4.5 1.0 %copy-start.4 = (bf16[768,256]{1,0:T(8,128)(2,1)S(1)}, bf16[768,256]{1,0:T(8,128)(2,1)}, u32[]{:S(2)}) copy-start(bf16[768,256]{1,0:T(8,128)(2,1)} %constant.12.clone.second) | copy-start | bytes 1179652
  5.5 0.9 %copy-start.5 = (bf16[1,512,256]{2,1,0:T(8,128)(2,1)S(1)}, bf16[1,512,256]{2,1,0:T(8,128)(2,1)}, u32[]{:S(2)}) copy-start(bf16[1,512,256]{2,1,0:T(8,128)(2,1)} %param.11) | copy-start | bytes 786436
  6.4 0.9 %copy-start.6 = (bf16[1,512,256]{2,1,0:T(8,128)(2,1)S(1)}, bf16[1,512,256]{2,1,0:T(8,128)(2,1)}, u32[]{:S(2)}) copy-start(bf16[1,512,256]{2,1,0:T(8,128)(2,1)} %param.12) | copy-start | bytes 786436
  7.4 0.9 %copy-start.7 = (bf16[512,256]{1,0:T(8,128)(2,1)S(1)}, bf16[512,256]{1,0:T(8,128)(2,1)}, u32[]{:S(2)}) copy-start(bf16[512,256]{1,0:T(8,128)(2,1)} %codes.1) | copy-start | bytes 786436
  8.3 0.9 %copy-start.8 = (f32[256,256]{1,0:T(8,128)S(1)}, f32[256,256]{1,0:T(8,128)}, u32[]{:S(2)}) copy-start(f32[256,256]{1,0:T(8,128)} %constant.11.clone.turn) | copy-start | bytes 786436
  9.3 56.7 %copy-start.2 = (s32[512,256]{1,0:T(8,128)S(1)}, s32[512,256]{1,0:T(8,128)}, u32[]{:S(2)}) copy-start(s32[512,256]{1,0:T(8,128)} %mask.1) | copy-start | bytes 1572868
where the time goes:
time: 67.7 us; the launch traced here: 67.3 us
  Pallas kernels  57.9 us (86%)
  local copies, waits for them, and re-layouts  8.65 us (13%)
    pallas_call x1, Pallas kernels, per_device(): pl.pallas_call(main_kernel, out_shape=jax.ShapeDtypeStruct((ALL, 2 * ROWS...  56.7 us
    unnamed x22, local copies, waits for them, and re-layouts  8.65 us

commit v1 on v0

v1 whole, which is shorter than its diff:
```python
import functools
import math

import jax
import jax.numpy as jnp
import numpy as np
from jax import lax
from jax.experimental import pallas as pl
from jax.experimental.pallas import tpu as pltpu
from jax.sharding import PartitionSpec as P

LOGICAL = pl.DeviceIdType.LOGICAL
F32 = jnp.float32
BF16 = jnp.bfloat16
LANES = 128
ROWS = 4
SEQ = 64
DP = 4
ALL = SEQ * DP
HALF = SEQ * ROWS
POINTS = 2 * HALF * LANES
VMEM_LIMIT = 58 << 20


def split(values):
    high = values.astype(BF16)
    return high, (values - high.astype(F32)).astype(BF16)


def np_split(values):
    values = values.astype(np.float32)
    high = values.astype(jnp.bfloat16)
    return high, (values - high.astype(np.float32)).astype(jnp.bfloat16)


def tables():
    rows = (ROWS * np.arange(SEQ)[None, :] + np.arange(ROWS)[:, None]).reshape(-1)
    odd = 2 * np.arange(HALF) + 1
    angle = 2 * np.pi / (4 * HALF) * ((odd[:, None] * rows[None, :]) % (4 * HALF))
    first = np.concatenate([np.cos(angle), -np.sin(angle)], axis=0)
    lane = np.arange(LANES)
    angle = 2 * np.pi / (2 * POINTS) * ((odd[:, None] * lane[None, :]) % (2 * POINTS))
    turn = np.concatenate([np.cos(angle), -np.sin(angle)], axis=1).astype(np.float32)
    angle = 2 * np.pi / LANES * ((lane[:, None] * lane[None, :]) % LANES)
    cos, sin = np.cos(angle), np.sin(angle)
    second = np.block([[cos, -sin], [sin, cos]])
    first_high, first_low = np_split(first)
    second_high, second_low = np_split(second)
    return (
        np.concatenate([first_high, first_low], axis=1),
        turn,
        np.concatenate([second_high, second_high, second_low], axis=0),
        np.concatenate([second_high.T, second_high.T, second_low.T], axis=0),
        np.concatenate([first_high.T, first_low.T, first_high.T], axis=1),
    )


def dot(left, right):
    return jnp.dot(left, right, preferred_element_type=F32)


def dot_nt(left, right):
    return lax.dot_general(left, right, (((1,), (1,)), ((), ())), preferred_element_type=F32)


def same(shape, offset=0, factor=1):
    row = lax.broadcasted_iota(jnp.int32, shape, 0)
    column = lax.broadcasted_iota(jnp.int32, shape, 1)
    return jnp.where(column == factor * row + offset, 1.0, 0.0).astype(BF16)


def mix(values, matrix):
    high, low = split(values)
    return dot(jnp.concatenate([high, low, high], axis=1), matrix)


def forward(rows, first, turn, second):
    both = dot(first, jnp.concatenate([rows, rows], axis=0))
    cos, sin = turn[:, :LANES], turn[:, LANES:]
    spectra = []
    for at in range(0, rows.shape[1], LANES):
        real, imag = both[:HALF, at : at + LANES], both[HALF:, at : at + LANES]
        turned = jnp.concatenate([real * cos - imag * sin, real * sin + imag * cos], axis=1)
        spectra.append(mix(turned, second))
    return spectra


def backward(spectra, turn, second_back, first_back):
    cos, sin = turn[:, :LANES], turn[:, LANES:]
    columns = []
    for spectrum in spectra:
        both = mix(spectrum, second_back)
        real, imag = both[:, :LANES], both[:, LANES:]
        columns.append(
            jnp.concatenate([real * cos + imag * sin, imag * cos - real * sin], axis=0)
        )
    high, low = split(jnp.concatenate(columns, axis=1))
    return dot(first_back, jnp.concatenate([high, high, low], axis=0))


def conj_product(left, right):
    left_real, left_imag = left[:, :LANES], left[:, LANES:]
    right_real, right_imag = right[:, :LANES], right[:, LANES:]
    return jnp.concatenate(
        [
            left_real * right_real + left_imag * right_imag,
            left_real * right_imag - left_imag * right_real,
        ],
        axis=1,
    )


def spread(wide, values, count):
    for row in range(ROWS):
        wide[pl.ds(0, count), row, :] = values[:, row * LANES : (row + 1) * LANES]
    return wide[pl.ds(0, count)].astype(BF16)


def gather(wide, start):
    return jnp.concatenate([wide[pl.ds(start, SEQ), row, :] for row in range(ROWS)], axis=0)


def main_kernel(
    signal_hbm, cotangent_hbm, codes_hbm, exponents, skip,
    first_hbm, turn_hbm, second_hbm, second_back_hbm, first_back_hbm,
    home_grad, home_total,
    signal, cotangent, codes, first, turn, second, second_back, first_back,
    wide, codes_out, cot_out, sig_out, codes_in, cot_in, sig_in, grad_out, total_out,
    cot_spec, send_sem, recv_sem, load_sem,
):
    loads = [
        pltpu.make_async_copy(source, target, load_sem.at[index])
        for index, (source, target) in enumerate(
            (
                (codes_hbm, codes), (cotangent_hbm, cotangent), (signal_hbm, signal),
                (first_hbm, first), (turn_hbm, turn), (second_hbm, second),
                (second_back_hbm, second_back), (first_back_hbm, first_back),
            )
        )
    ]
    for load in loads:
        load.start()
    s, d = lax.axis_index("seq"), lax.axis_index("dp")
    me = s * DP + d
    place = d * SEQ + s
    barrier = pltpu.get_barrier_semaphore()

    def greet(step, carry):
        other = lax.rem(me + step, ALL)
        pl.semaphore_signal(barrier, inc=1, device_id=other, device_id_type=LOGICAL)
        return carry

    lax.fori_loop(1, ALL, greet, 0, unroll=15)

    def post(index, source, target, other):
        pltpu.make_async_remote_copy(
            src_ref=source, dst_ref=target,
            send_sem=send_sem.at[index], recv_sem=recv_sem.at[index],
            device_id=other, device_id_type=LOGICAL,
        ).start()

    def drain(index, array, count):
        part = array.at[pl.ds(0, count)]
        return pltpu.make_async_remote_copy(
            src_ref=part, dst_ref=part,
            send_sem=send_sem.at[index], recv_sem=recv_sem.at[index],
            device_id=me, device_id_type=LOGICAL,
        )

    loads[0].wait()
    codes_out[...] = spread(wide, dot_nt(same((SEQ, ALL), d, DP), codes[...]), SEQ)
    loads[1].wait()
    eye = same((ALL, ALL))
    cot_out[...] = spread(wide, dot_nt(eye, cotangent[...]), ALL)
    pl.semaphore_wait(barrier, ALL - 1)

    def send_codes(step, carry):
        other = lax.rem(s + step, SEQ)
        post(0, codes_out.at[other], codes_in.at[s], other * DP + d)
        return carry

    lax.fori_loop(1, SEQ, send_codes, 0, unroll=9)

    def send_cot(step, carry):
        other = lax.rem(me + step, ALL)
        post(1, cot_out.at[other], cot_in.at[place], other)
        return carry

    lax.fori_loop(1, ALL, send_cot, 0, unroll=15)

    loads[2].wait()
    sig_out[...] = spread(wide, dot_nt(eye, signal[...]), ALL)

    def send_sig(step, carry):
        other = lax.rem(me + step, ALL)
        post(2, sig_out.at[other], sig_in.at[place], other)
        return carry

    lax.fori_loop(1, ALL, send_sig, 0, unroll=15)
    codes_in[pl.ds(s, 1)] = codes_out[pl.ds(s, 1)]
    cot_in[pl.ds(place, 1)] = cot_out[pl.ds(me, 1)]
    sig_in[pl.ds(place, 1)] = sig_out[pl.ds(me, 1)]
    for load in loads[3:]:
        load.wait()
    unit = jnp.full((1, LANES), exponents[me].astype(F32), F32)
    scale = jnp.exp2(unit) * (2.0 / POINTS)
    direct = skip[me]

    drain(0, codes_in, SEQ - 1).wait_recv()
    wide[pl.ds(0, SEQ)] = codes_in[...].astype(F32)
    (codes_spec,) = forward(gather(wide, 0).astype(BF16), first[...], turn[...], second[...])

    drain(1, cot_in, ALL - 1).wait_recv()
    wide[...] = cot_in[...].astype(F32)
    for pair in (0, 2):
        dps = [lax.rem(d + pair + index, DP) for index in range(2)]
        cots = [gather(wide, which * SEQ) for which in dps]
        both = jnp.concatenate(cots, axis=1)
        spectra = forward(both.astype(BF16), first[...], turn[...], second[...])
        for index, spectrum in enumerate(spectra):
            cot_spec[pair + index] = spectrum
        back = backward(
            [conj_product(codes_spec, spectrum) for spectrum in spectra],
            turn[...], second_back[...], first_back[...],
        )
        for index, which in enumerate(dps):
            grad = back[:, index * LANES : (index + 1) * LANES] * scale + direct * cots[index]
            for row in range(ROWS):
                wide[pl.ds(which * SEQ, SEQ), row, :] = grad[row * SEQ : (row + 1) * SEQ]
            grad_out[pl.ds(which * SEQ, SEQ)] = wide[pl.ds(which * SEQ, SEQ)].astype(BF16)

            def send_grad(step, carry, which=which):
                to_seq = lax.rem(s + step, SEQ)
                post(3, grad_out.at[which * SEQ + to_seq], home_grad.at[me], to_seq * DP + which)
                return carry

            if pair + index == 0:
                home_grad[pl.ds(me, 1)] = grad_out[pl.ds(place, 1)]
                lax.fori_loop(1, SEQ, send_grad, 0, unroll=9)
            else:
                lax.fori_loop(0, SEQ, send_grad, 0, unroll=8)

    drain(2, sig_in, ALL - 1).wait_recv()
    wide[...] = sig_in[...].astype(F32)
    total_spec = jnp.zeros((HALF, 2 * LANES), F32)
    for pair in (0, 2):
        dps = [lax.rem(d + pair + index, DP) for index in range(2)]
        both = jnp.concatenate([gather(wide, which * SEQ) for which in dps], axis=1)
        spectra = forward(both.astype(BF16), first[...], turn[...], second[...])
        for index, spectrum in enumerate(spectra):
            total_spec += conj_product(spectrum, cot_spec[pair + index])
    total = backward([total_spec], turn[...], second_back[...], first_back[...])
    total = total * (2.0 / POINTS)
    for row in range(ROWS):
        wide[pl.ds(0, SEQ), row, :] = total[row * SEQ : (row + 1) * SEQ]
    total_out[...] = wide[pl.ds(0, SEQ)].astype(BF16)

    def send_total(step, carry):
        other = lax.rem(me + step, ALL)
        post(4, total_out.at[other // DP], home_total.at[me], other)
        return carry

    lax.fori_loop(1, ALL, send_total, 0, unroll=15)
    home_total[pl.ds(me, 1)] = total_out[pl.ds(s, 1)]
    drain(0, codes_out, SEQ - 1).wait_send()
    drain(1, cot_out, ALL - 1).wait_send()
    drain(2, sig_out, ALL - 1).wait_send()
    drain(3, grad_out, ALL - 1).wait_send()
    drain(4, home_total, ALL - 1).wait_send()
    drain(3, home_grad, ALL - 1).wait_recv()
    drain(4, home_total, ALL - 1).wait_recv()


def last_kernel(home_grad, home_total, mask_hbm, exponents, input_grad, filter_grad, wide, mask, load_sem):
    load = pltpu.make_async_copy(mask_hbm, mask, load_sem)
    load.start()
    eye = same((LANES, LANES))
    wide[...] = home_grad[...].astype(F32)
    for row in range(ROWS):
        part = pl.ds(row * LANES, LANES)
        input_grad[part, :] = dot_nt(eye, wide[:, row, :].astype(BF16)).astype(BF16)
    scale = jnp.exp2(exponents[...].astype(F32)) * (1.0 / math.sqrt(DP * HALF * LANES))
    wide[...] = home_total[...].astype(F32)
    load.wait()
    for row in range(ROWS):
        part = pl.ds(row * LANES, LANES)
        total = dot_nt(eye, wide[:, row, :].astype(BF16))
        filter_grad[part, :] = mask[part, :].astype(F32) * scale * total


def per_device(signal, cotangent, filter_codes, keep_mask, exponents, skip):
    span, width = signal.shape[1], signal.shape[2]
    vmem = pl.BlockSpec(memory_space=pltpu.VMEM)
    smem = pl.BlockSpec(memory_space=pltpu.SMEM)
    hbm = pl.BlockSpec(memory_space=pltpu.HBM)
    constants = [jnp.asarray(table) for table in tables()]
    message = (ROWS, LANES)
    home_grad, home_total = pl.pallas_call(
        main_kernel,
        out_shape=(jax.ShapeDtypeStruct((ALL,) + message, BF16),) * 2,
        in_specs=[hbm] * 3 + [smem] * 2 + [hbm] * 5,
        out_specs=(vmem, vmem),
        scratch_shapes=[
            pltpu.VMEM((span, width), BF16),
            pltpu.VMEM((span, width), BF16),
            pltpu.VMEM((span, width), BF16),
            *[pltpu.VMEM(table.shape, table.dtype) for table in constants],
            pltpu.VMEM((ALL,) + message, F32),
            pltpu.VMEM((SEQ,) + message, BF16),
            pltpu.VMEM((ALL,) + message, BF16),
            pltpu.VMEM((ALL,) + message, BF16),
            pltpu.VMEM((SEQ,) + message, BF16),
            pltpu.VMEM((ALL,) + message, BF16),
            pltpu.VMEM((ALL,) + message, BF16),
            pltpu.VMEM((ALL,) + message, BF16),
            pltpu.VMEM((SEQ,) + message, BF16),
            pltpu.VMEM((DP, HALF, 2 * LANES), F32),
            pltpu.SemaphoreType.DMA((5,)),
            pltpu.SemaphoreType.DMA((5,)),
            pltpu.SemaphoreType.DMA((8,)),
        ],
        compiler_params=pltpu.CompilerParams(
            collective_id=0, has_side_effects=True, vmem_limit_bytes=VMEM_LIMIT
        ),
        name="main",
    )(
        signal.reshape(span, width), cotangent.reshape(span, width), filter_codes,
        exponents, skip, *constants,
    )
    input_grad, filter_grad = pl.pallas_call(
        last_kernel,
        out_shape=(
            jax.ShapeDtypeStruct((span, width), BF16),
            jax.ShapeDtypeStruct((span, width), F32),
        ),
        in_specs=[vmem, vmem, hbm, vmem],
        out_specs=(vmem, vmem),
        scratch_shapes=[
            pltpu.VMEM((ALL,) + message, F32),
            pltpu.VMEM((span, width), jnp.int32),
            pltpu.SemaphoreType.DMA,
        ],
        compiler_params=pltpu.CompilerParams(vmem_limit_bytes=VMEM_LIMIT),
        name="last",
    )(home_grad, home_total, keep_mask, exponents.reshape(1, width))
    return input_grad.reshape(signal.shape), filter_grad


def solution(mesh):
    return jax.shard_map(
        per_device,
        mesh=mesh,
        in_specs=(
            P("dp", "seq", None),
            P("dp", "seq", None),
            P("seq", None),
            P("seq", None),
            P(),
            P(),
        ),
        out_specs=(P("dp", "seq", None), P("seq", None)),
        check_vma=False,
    )
```

time: 67.7 us -> 51.7 us (0.76)
  local copies, waits for them, and re-layouts: 8.65 us -> 0 us
  Pallas kernels: 57.9 us -> 50.9 us
    pallas_call x1, Pallas kernels: 56.7 us -> 47.3 us  [per_device(): pl.pallas_call(main_kernel, out_shape=(jax.ShapeDtypeStruct((ALL,) + mess...]
    unnamed x22 -> x0, local copies, waits for them, and re-layouts: 8.65 us -> none
    pallas_call x1, Pallas kernels: 1.26 us -> 3.6 us  [per_device(): pl.pallas_call(last_kernel, out_shape=(jax.ShapeDtypeStruct((span, width)...]
where the time goes in v1:
time: 51.7 us; the launch traced here: 51.6 us
  Pallas kernels  50.9 us (98%)
  between operations  0.64 us (1%)
    pallas_call x1, Pallas kernels, per_device(): pl.pallas_call(main_kernel, out_shape=(jax.ShapeDtypeStruct((ALL,) + mess...  47.3 us
    pallas_call x1, Pallas kernels, per_device(): pl.pallas_call(last_kernel, out_shape=(jax.ShapeDtypeStruct((span, width)...  3.6 us

profile of v1, /device:TPU:1, one launch (start us, length us, event | category | flops | bytes accessed | tf_op | source)
XLA Modules:
  0.0 51.6 jit_solution(14472272288401360551)
XLA Ops:
  0.6 47.3 %main.1 = (bf16[256,4,128]{2,1,0:T(4,128)(2,1)}, bf16[256,4,128]{2,1,0:T(4,128)(2,1)}) custom-call(bf16[512,256]{1,0:T(8,128)(2,1)} %bitcast.4, bf16[512,256]{1,0:T(8,128)(2,1)} %bitcast.5, bf16[512,256]{1,0:T(8,128)(2,1)} %codes_hbm.1, s32[256]{0:T(256)} %exponents.1, f32[256]{0:T(256)} %skip.1, bf16[512,512]{1,0:T(8,128)(2,1)} %constant.10.clone.first_hbm, ...), custom_call_target="tpu_custom_call" | custom-call | tf_op jit(solution)/shard_map/main/pallas_call | solution.py:298
  48.0 3.6 %last.1 = (bf16[512,256]{1,0:T(8,128)(2,1)}, f32[512,256]{1,0:T(8,128)}) custom-call(bf16[256,4,128]{2,1,0:T(4,128)(2,1)} %get-tuple-element.6.home_grad, bf16[256,4,128]{2,1,0:T(4,128)(2,1)} %get-tuple-element.7.home_total, s32[512,256]{1,0:T(8,128)} %mask_hbm.1, s32[1,256]{1,0:T(1,128)} %bitcast.6), custom_call_target="tpu_custom_call" | custom-call | tf_op jit(solution)/shard_map/last/pallas_call | solution.py:330

commit v2 on v1

v2 whole, which is shorter than its diff:
```python
import functools
import math

import jax
import jax.numpy as jnp
import numpy as np
from jax import lax
from jax.experimental import pallas as pl
from jax.experimental.pallas import tpu as pltpu
from jax.sharding import PartitionSpec as P

LOGICAL = pl.DeviceIdType.LOGICAL
F32 = jnp.float32
BF16 = jnp.bfloat16
LANES = 128
ROWS = 4
SEQ = 64
DP = 4
ALL = SEQ * DP
HALF = SEQ * ROWS
POINTS = 2 * HALF * LANES
Z, X, Y = 8, 4, 2
VMEM_LIMIT = 58 << 20


def split(values):
    high = values.astype(BF16)
    return high, (values - high.astype(F32)).astype(BF16)


def np_split(values):
    values = values.astype(np.float32)
    high = values.astype(jnp.bfloat16)
    return high, (values - high.astype(np.float32)).astype(jnp.bfloat16)


def tables():
    rows = (ROWS * np.arange(SEQ)[None, :] + np.arange(ROWS)[:, None]).reshape(-1)
    odd = 2 * np.arange(HALF) + 1
    angle = 2 * np.pi / (4 * HALF) * ((odd[:, None] * rows[None, :]) % (4 * HALF))
    first = np.concatenate([np.cos(angle), -np.sin(angle)], axis=0)
    lane = np.arange(LANES)
    angle = 2 * np.pi / (2 * POINTS) * ((odd[:, None] * lane[None, :]) % (2 * POINTS))
    turn = np.concatenate([np.cos(angle), -np.sin(angle)], axis=1).astype(np.float32)
    angle = 2 * np.pi / LANES * ((lane[:, None] * lane[None, :]) % LANES)
    cos, sin = np.cos(angle), np.sin(angle)
    second = np.block([[cos, -sin], [sin, cos]])
    first_high, first_low = np_split(first)
    second_high, second_low = np_split(second)
    return (
        np.concatenate([first_high, first_low], axis=1),
        turn,
        np.concatenate([second_high, second_high, second_low], axis=0),
        np.concatenate([second_high.T, second_high.T, second_low.T], axis=0),
        np.concatenate([first_high.T, first_low.T, first_high.T], axis=1),
    )


def dot(left, right):
    return jnp.dot(left, right, preferred_element_type=F32)


def dot_nt(left, right):
    return lax.dot_general(left, right, (((1,), (1,)), ((), ())), preferred_element_type=F32)


def same(shape, offset=0, factor=1):
    row = lax.broadcasted_iota(jnp.int32, shape, 0)
    column = lax.broadcasted_iota(jnp.int32, shape, 1)
    return jnp.where(column == factor * row + offset, 1.0, 0.0).astype(BF16)


def mix(values, matrix):
    high, low = split(values)
    return dot(jnp.concatenate([high, low, high], axis=1), matrix)


def forward(rows, first, turn, second):
    both = dot(first, jnp.concatenate([rows, rows], axis=0))
    cos, sin = turn[:, :LANES], turn[:, LANES:]
    spectra = []
    for at in range(0, rows.shape[1], LANES):
        real, imag = both[:HALF, at : at + LANES], both[HALF:, at : at + LANES]
        turned = jnp.concatenate([real * cos - imag * sin, real * sin + imag * cos], axis=1)
        spectra.append(mix(turned, second))
    return spectra


def backward(spectra, turn, second_back, first_back):
    cos, sin = turn[:, :LANES], turn[:, LANES:]
    columns = []
    for spectrum in spectra:
        both = mix(spectrum, second_back)
        real, imag = both[:, :LANES], both[:, LANES:]
        columns.append(
            jnp.concatenate([real * cos + imag * sin, imag * cos - real * sin], axis=0)
        )
    high, low = split(jnp.concatenate(columns, axis=1))
    return dot(first_back, jnp.concatenate([high, high, low], axis=0))


def conj_product(left, right):
    left_real, left_imag = left[:, :LANES], left[:, LANES:]
    right_real, right_imag = right[:, :LANES], right[:, LANES:]
    return jnp.concatenate(
        [
            left_real * right_real + left_imag * right_imag,
            left_real * right_imag - left_imag * right_real,
        ],
        axis=1,
    )


def hops(near):
    def distance(step):
        up, across, along, side, _ = step
        return min(along, Z - along) + min(across, X - across) + (2 * up + side) % 3 + up * side

    steps = [
        (up, across, along, side, core)
        for along in range(Z)
        for across in range(X)
        for up in range(Y)
        for side, core in near
    ]
    steps.sort(key=lambda step: -distance(step))
    return steps


DP_STEPS = ((0, 0), (0, 1), (1, 0), (1, 1))


def spread(wide, values, count):
    for row in range(ROWS):
        wide[pl.ds(0, count), row, :] = values[:, row * LANES : (row + 1) * LANES]
    return wide[pl.ds(0, count)].astype(BF16)


def gather(wide, start):
    return jnp.concatenate([wide[pl.ds(start, SEQ), row, :] for row in range(ROWS)], axis=0)


def main_kernel(
    signal_hbm, cotangent_hbm, codes_hbm, mask_hbm, exponents, skip, powers_hbm,
    first_hbm, turn_hbm, second_hbm, second_back_hbm, first_back_hbm,
    input_hbm, filter_hbm,
    signal, cotangent, codes, mask, powers, first, turn, second, second_back, first_back,
    wide, codes_out, cot_out, sig_out, codes_in, cot_in, sig_in, grad_out, total_out,
    home_grad, home_total, input_grad, filter_grad,
    cot_spec, send_sem, recv_sem, load_sem, store_sem,
):
    loads = [
        pltpu.make_async_copy(source, target, load_sem.at[index])
        for index, (source, target) in enumerate(
            (
                (codes_hbm, codes), (cotangent_hbm, cotangent), (signal_hbm, signal),
                (first_hbm, first), (turn_hbm, turn), (second_hbm, second),
                (second_back_hbm, second_back), (first_back_hbm, first_back),
                (powers_hbm, powers), (mask_hbm, mask),
            )
        )
    ]
    for load in loads:
        load.start()
    s, d = lax.axis_index("seq"), lax.axis_index("dp")
    me = s * DP + d
    side, core = d // 2, lax.rem(d, 2)
    q = core * 2 + side
    place = q * SEQ + s
    along = [lax.rem(s + step, Z) for step in range(Z)]
    across = [lax.rem(s // Z + step, X) * Z for step in range(X)]
    up = [lax.rem(s // (Z * X) + step, Y) * (Z * X) for step in range(Y)]
    sides = [lax.rem(side + step, 2) for step in range(2)]
    cores = [lax.rem(core + step, 2) for step in range(2)]

    def target(step):
        to_seq = up[step[0]] + across[step[1]] + along[step[2]]
        to_side, to_core = sides[step[3]], cores[step[4]]
        return to_seq, to_core * 2 + to_side, to_seq * DP + to_side * 2 + to_core

    everyone = [step for step in hops(DP_STEPS) if any(step)]
    barrier = pltpu.get_barrier_semaphore()
    for step in everyone:
        pl.semaphore_signal(barrier, inc=1, device_id=target(step)[2], device_id_type=LOGICAL)

    def post(index, source, destination, other):
        pltpu.make_async_remote_copy(
            src_ref=source, dst_ref=destination,
            send_sem=send_sem.at[index], recv_sem=recv_sem.at[index],
            device_id=other, device_id_type=LOGICAL,
        ).start()

    def drain(index, array, count):
        part = array.at[pl.ds(0, count)]
        return pltpu.make_async_remote_copy(
            src_ref=part, dst_ref=part,
            send_sem=send_sem.at[index], recv_sem=recv_sem.at[index],
            device_id=me, device_id_type=LOGICAL,
        )

    loads[0].wait()
    codes_out[...] = spread(wide, dot_nt(same((SEQ, ALL), q * SEQ), codes[...]), SEQ)
    loads[1].wait()
    eye = same((ALL, ALL))
    cot_out[...] = spread(wide, dot_nt(eye, cotangent[...]), ALL)
    pl.semaphore_wait(barrier, ALL - 1)

    for step in hops(((0, 0),)):
        if any(step):
            to_seq, _, other = target(step)
            post(0, codes_out.at[to_seq], codes_in.at[s], other)
    for step in everyone:
        to_seq, to_q, other = target(step)
        post(1, cot_out.at[to_q * SEQ + to_seq], cot_in.at[place], other)

    loads[2].wait()
    sig_out[...] = spread(wide, dot_nt(eye, signal[...]), ALL)
    for step in everyone:
        to_seq, to_q, other = target(step)
        post(2, sig_out.at[to_q * SEQ + to_seq], sig_in.at[place], other)
    codes_in[pl.ds(s, 1)] = codes_out[pl.ds(s, 1)]
    cot_in[pl.ds(place, 1)] = cot_out[pl.ds(place, 1)]
    sig_in[pl.ds(place, 1)] = sig_out[pl.ds(place, 1)]
    for load in loads[3:]:
        load.wait()
    unit = jnp.full((1, LANES), exponents[place].astype(F32), F32)
    scale = jnp.exp2(unit) * (2.0 / POINTS)
    direct = skip[place]

    drain(0, codes_in, SEQ - 1).wait_recv()
    wide[pl.ds(0, SEQ)] = codes_in[...].astype(F32)
    (codes_spec,) = forward(gather(wide, 0).astype(BF16), first[...], turn[...], second[...])

    drain(1, cot_in, ALL - 1).wait_recv()
    wide[...] = cot_in[...].astype(F32)
    for pair in (0, 2):
        near = DP_STEPS[pair : pair + 2]
        which = [cores[step[1]] * 2 + sides[step[0]] for step in near]
        cots = [gather(wide, index * SEQ) for index in which]
        both = jnp.concatenate(cots, axis=1)
        spectra = forward(both.astype(BF16), first[...], turn[...], second[...])
        for index, spectrum in enumerate(spectra):
            cot_spec[pair + index] = spectrum
        back = backward(
            [conj_product(codes_spec, spectrum) for spectrum in spectra],
            turn[...], second_back[...], first_back[...],
        )
        for index in range(2):
            grad = back[:, index * LANES : (index + 1) * LANES] * scale + direct * cots[index]
            part = pl.ds(which[index] * SEQ, SEQ)
            for row in range(ROWS):
                wide[part, row, :] = grad[row * SEQ : (row + 1) * SEQ]
            grad_out[part] = wide[part].astype(BF16)
            for step in hops((near[index],)):
                if any(step):
                    to_seq, to_q, other = target(step)
                    post(3, grad_out.at[to_q * SEQ + to_seq], home_grad.at[place], other)

    drain(2, sig_in, ALL - 1).wait_recv()
    wide[...] = sig_in[...].astype(F32)
    total_spec = jnp.zeros((HALF, 2 * LANES), F32)
    for pair in (0, 2):
        near = DP_STEPS[pair : pair + 2]
        which = [cores[step[1]] * 2 + sides[step[0]] for step in near]
        both = jnp.concatenate([gather(wide, index * SEQ) for index in which], axis=1)
        spectra = forward(both.astype(BF16), first[...], turn[...], second[...])
        for index, spectrum in enumerate(spectra):
            total_spec += conj_product(spectrum, cot_spec[pair + index])
    total = backward([total_spec], turn[...], second_back[...], first_back[...])
    total = total * (2.0 / POINTS)
    for row in range(ROWS):
        wide[pl.ds(0, SEQ), row, :] = total[row * SEQ : (row + 1) * SEQ]
    total_out[...] = wide[pl.ds(0, SEQ)].astype(BF16)
    for step in hops(((0, 0), (1, 0))):
        if any(step):
            to_seq, _, other = target(step)
            post(4, total_out.at[to_seq], home_total.at[place], other)
    home_total[pl.ds(place, 1)] = total_out[pl.ds(s, 1)]
    home_grad[pl.ds(place, 1)] = grad_out[pl.ds(place, 1)]

    eye = same((LANES, LANES))
    drain(3, home_grad, ALL - 1).wait_recv()
    wide[...] = home_grad[...].astype(F32)
    for row in range(ROWS):
        grad = wide[:, row, :].astype(BF16)
        input_grad[pl.ds(row * LANES, LANES), :] = dot_nt(eye, grad).astype(BF16)
    store_input = pltpu.make_async_copy(input_grad, input_hbm, store_sem.at[0])
    store_input.start()

    half = 2 * SEQ
    drain(4, home_total, half - 1).wait_recv()
    mine = home_total.at[pl.ds(core * half, half)]
    across_core = pltpu.make_async_remote_copy(
        src_ref=mine, dst_ref=mine, send_sem=send_sem.at[5], recv_sem=recv_sem.at[5],
        device_id=me + 1 - 2 * core, device_id_type=LOGICAL,
    )
    across_core.start()
    factor = jnp.exp2(powers[...].astype(F32)) * (1.0 / math.sqrt(DP * HALF * LANES))

    def finish(which):
        channels = pl.ds(pl.multiple_of(which * half, LANES), half)
        wide[pl.ds(0, half)] = home_total[pl.ds(which * half, half)].astype(F32)
        chosen = jnp.where(which == 0, factor[:, :half], factor[:, half:])
        for row in range(ROWS):
            part = pl.ds(row * LANES, LANES)
            value = dot_nt(eye, wide[pl.ds(0, half), row, :].astype(BF16))
            filter_grad[part, channels] = mask[part, channels].astype(F32) * chosen * value

    finish(core)
    across_core.wait_recv()
    finish(1 - core)
    store_filter = pltpu.make_async_copy(filter_grad, filter_hbm, store_sem.at[1])
    store_filter.start()
    drain(0, codes_out, SEQ - 1).wait_send()
    drain(1, cot_out, ALL - 1).wait_send()
    drain(2, sig_out, ALL - 1).wait_send()
    drain(3, grad_out, ALL - 1).wait_send()
    drain(4, home_total, half - 1).wait_send()
    across_core.wait_send()
    store_input.wait()
    store_filter.wait()


def last_kernel(input_main, filter_main, input_grad, filter_grad, input_held, filter_held, sem):
    steps = []
    for source, held, result in (
        (filter_main, filter_held, filter_grad), (input_main, input_held, input_grad)
    ):
        size = source.shape[0] // 4
        for index in range(4):
            part = pl.ds(index * size, size)
            at = len(steps)
            steps.append(
                (
                    pltpu.make_async_copy(source.at[part], held.at[part], sem.at[0, at]),
                    pltpu.make_async_copy(held.at[part], result.at[part], sem.at[1, at]),
                )
            )
    for load, _ in steps:
        load.start()
    for load, store in steps:
        load.wait()
        store.start()
    for _, store in steps:
        store.wait()


def per_device(signal, cotangent, filter_codes, keep_mask, exponents, skip):
    span, width = signal.shape[1], signal.shape[2]
    smem = pl.BlockSpec(memory_space=pltpu.SMEM)
    hbm = pl.BlockSpec(memory_space=pltpu.HBM)
    constants = [jnp.asarray(table) for table in tables()]
    message = (ROWS, LANES)
    results = (
        jax.ShapeDtypeStruct((span, width), BF16),
        jax.ShapeDtypeStruct((span, width), F32),
    )
    input_main, filter_main = pl.pallas_call(
        main_kernel,
        out_shape=results,
        in_specs=[hbm] * 4 + [smem] * 2 + [hbm] * 6,
        out_specs=(hbm, hbm),
        scratch_shapes=[
            pltpu.VMEM((span, width), BF16),
            pltpu.VMEM((span, width), BF16),
            pltpu.VMEM((span, width), BF16),
            pltpu.VMEM((span, width), jnp.int32),
            pltpu.VMEM((1, width), jnp.int32),
            *[pltpu.VMEM(table.shape, table.dtype) for table in constants],
            pltpu.VMEM((ALL,) + message, F32),
            pltpu.VMEM((SEQ,) + message, BF16),
            pltpu.VMEM((ALL,) + message, BF16),
            pltpu.VMEM((ALL,) + message, BF16),
            pltpu.VMEM((SEQ,) + message, BF16),
            pltpu.VMEM((ALL,) + message, BF16),
            pltpu.VMEM((ALL,) + message, BF16),
            pltpu.VMEM((ALL,) + message, BF16),
            pltpu.VMEM((SEQ,) + message, BF16),
            pltpu.VMEM((ALL,) + message, BF16),
            pltpu.VMEM((ALL,) + message, BF16),
            pltpu.VMEM((span, width), BF16),
            pltpu.VMEM((span, width), F32),
            pltpu.VMEM((DP, HALF, 2 * LANES), F32),
            pltpu.SemaphoreType.DMA((6,)),
            pltpu.SemaphoreType.DMA((6,)),
            pltpu.SemaphoreType.DMA((10,)),
            pltpu.SemaphoreType.DMA((2,)),
        ],
        compiler_params=pltpu.CompilerParams(
            collective_id=0, has_side_effects=True, vmem_limit_bytes=VMEM_LIMIT
        ),
        name="main",
    )(
        signal.reshape(span, width), cotangent.reshape(span, width), filter_codes, keep_mask,
        exponents, skip, exponents.reshape(1, width), *constants,
    )
    input_grad, filter_grad = pl.pallas_call(
        last_kernel,
        out_shape=results,
        in_specs=[hbm, hbm],
        out_specs=(hbm, hbm),
        scratch_shapes=[
            pltpu.VMEM((span, width), BF16),
            pltpu.VMEM((span, width), F32),
            pltpu.SemaphoreType.DMA((2, 8)),
        ],
        compiler_params=pltpu.CompilerParams(vmem_limit_bytes=VMEM_LIMIT),
        name="last",
    )(input_main, filter_main)
    return input_grad.reshape(signal.shape), filter_grad


def solution(mesh):
    return jax.shard_map(
        per_device,
        mesh=mesh,
        in_specs=(
            P("dp", "seq", None),
            P("dp", "seq", None),
            P("seq", None),
            P("seq", None),
            P(),
            P(),
        ),
        out_specs=(P("dp", "seq", None), P("seq", None)),
        check_vma=False,
    )
```

time: 51.7 us -> 46.7 us (0.903)
  Pallas kernels: 50.9 us -> 46 us
    pallas_call x2, Pallas kernels: 50.9 us -> 46 us  [the longest x1 44 us: per_device(): pl.pallas_call(main_kernel, out_shape=results, in_specs=[hbm] * 4 + [smem...]
where the time goes in v2:
time: 46.7 us; the launch traced here: 46.6 us
  Pallas kernels  46 us (99%)
  between operations  0.64 us (1%)
    pallas_call x1, Pallas kernels, per_device(): pl.pallas_call(main_kernel, out_shape=results, in_specs=[hbm] * 4 + [smem...  44 us
    pallas_call x1, Pallas kernels, per_device(): pl.pallas_call(last_kernel, out_shape=results, in_specs=[hbm, hbm], out_s...  1.97 us

profile of v2, /device:TPU:1, one launch (start us, length us, event | category | flops | bytes accessed | tf_op | source)
XLA Modules:
  0.0 46.6 jit_solution(16358813320821585650)
XLA Ops:
  0.6 44.0 %main.1 = (bf16[512,256]{1,0:T(8,128)(2,1)}, f32[512,256]{1,0:T(8,128)}) custom-call(bf16[512,256]{1,0:T(8,128)(2,1)} %bitcast.4, bf16[512,256]{1,0:T(8,128)(2,1)} %bitcast.5, bf16[512,256]{1,0:T(8,128)(2,1)} %codes_hbm.1, s32[512,256]{1,0:T(8,128)} %mask_hbm.1, s32[256]{0:T(256)} %exponents.1, f32[256]{0:T(256)} %skip.1, s32[1,256]{1,0:T(1,128)} %bitcast.6, ...), custom_call_target="tpu_custom_call" | custom-call | tf_op jit(solution)/shard_map/main/pallas_call | solution.py:358
  44.6 2.0 %last.1 = (bf16[512,256]{1,0:T(8,128)(2,1)}, f32[512,256]{1,0:T(8,128)}) custom-call(bf16[512,256]{1,0:T(8,128)(2,1)} %get-tuple-element.6.input_main, f32[512,256]{1,0:T(8,128)} %get-tuple-element.7.filter_main), custom_call_target="tpu_custom_call" | custom-call | tf_op jit(solution)/shard_map/last/pallas_call | solution.py:397

commit v3 on v2

--- a/solution.py
+++ b/solution.py
@@ -111,10 +111,15 @@
     )
 
 
+EARLY = 191
+DP_STEPS = ((1, 1), (1, 0), (0, 1), (0, 0))
+
+
 def hops(near):
     def distance(step):
         up, across, along, side, _ = step
-        return min(along, Z - along) + min(across, X - across) + (2 * up + side) % 3 + up * side
+        turns = min(across, X - across) + ((0, 1), (2, 1))[up][side]
+        return 2 * turns + min(along, Z - along)
 
     steps = [
         (up, across, along, side, core)
@@ -125,9 +130,6 @@
     ]
     steps.sort(key=lambda step: -distance(step))
     return steps
-
-
-DP_STEPS = ((0, 0), (0, 1), (1, 0), (1, 1))
 
 
 def spread(wide, values, count):
@@ -173,10 +175,21 @@
     sides = [lax.rem(side + step, 2) for step in range(2)]
     cores = [lax.rem(core + step, 2) for step in range(2)]
 
+    seq_at = {
+        (a, b, c): up[a] + across[b] + along[c]
+        for a in range(Y) for b in range(X) for c in range(Z)
+    }
+    first_at = {step: to_seq * DP for step, to_seq in seq_at.items()}
+    dp_at = {
+        (a, b): (cores[b] * 2 + sides[a], sides[a] * 2 + cores[b])
+        for a in range(2) for b in range(2)
+    }
+    place_at = {near: to_q * SEQ for near, (to_q, _) in dp_at.items()}
+
     def target(step):
-        to_seq = up[step[0]] + across[step[1]] + along[step[2]]
-        to_side, to_core = sides[step[3]], cores[step[4]]
-        return to_seq, to_core * 2 + to_side, to_seq * DP + to_side * 2 + to_core
+        seq_step, near = step[:3], step[3:]
+        to_seq = seq_at[seq_step]
+        return to_seq, place_at[near] + to_seq, first_at[seq_step] + dp_at[near][1]
 
     everyone = [step for step in hops(DP_STEPS) if any(step)]
     barrier = pltpu.get_barrier_semaphore()
@@ -210,14 +223,14 @@
             to_seq, _, other = target(step)
             post(0, codes_out.at[to_seq], codes_in.at[s], other)
     for step in everyone:
-        to_seq, to_q, other = target(step)
-        post(1, cot_out.at[to_q * SEQ + to_seq], cot_in.at[place], other)
+        _, to_place, other = target(step)
+        post(1, cot_out.at[to_place], cot_in.at[place], other)
 
     loads[2].wait()
     sig_out[...] = spread(wide, dot_nt(eye, signal[...]), ALL)
     for step in everyone:
-        to_seq, to_q, other = target(step)
-        post(2, sig_out.at[to_q * SEQ + to_seq], sig_in.at[place], other)
+        _, to_place, other = target(step)
+        post(2, sig_out.at[to_place], sig_in.at[place], other)
     codes_in[pl.ds(s, 1)] = codes_out[pl.ds(s, 1)]
     cot_in[pl.ds(place, 1)] = cot_out[pl.ds(place, 1)]
     sig_in[pl.ds(place, 1)] = sig_out[pl.ds(place, 1)]
@@ -233,39 +246,35 @@
 
     drain(1, cot_in, ALL - 1).wait_recv()
     wide[...] = cot_in[...].astype(F32)
-    for pair in (0, 2):
-        near = DP_STEPS[pair : pair + 2]
-        which = [cores[step[1]] * 2 + sides[step[0]] for step in near]
-        cots = [gather(wide, index * SEQ) for index in which]
-        both = jnp.concatenate(cots, axis=1)
-        spectra = forward(both.astype(BF16), first[...], turn[...], second[...])
-        for index, spectrum in enumerate(spectra):
-            cot_spec[pair + index] = spectrum
-        back = backward(
-            [conj_product(codes_spec, spectrum) for spectrum in spectra],
-            turn[...], second_back[...], first_back[...],
-        )
-        for index in range(2):
-            grad = back[:, index * LANES : (index + 1) * LANES] * scale + direct * cots[index]
-            part = pl.ds(which[index] * SEQ, SEQ)
-            for row in range(ROWS):
-                wide[part, row, :] = grad[row * SEQ : (row + 1) * SEQ]
-            grad_out[part] = wide[part].astype(BF16)
-            for step in hops((near[index],)):
-                if any(step):
-                    to_seq, to_q, other = target(step)
-                    post(3, grad_out.at[to_q * SEQ + to_seq], home_grad.at[place], other)
+    cots = [gather(wide, index * SEQ) for index in range(DP)]
+    spectra = forward(
+        jnp.concatenate(cots, axis=1).astype(BF16), first[...], turn[...], second[...]
+    )
+    for index, spectrum in enumerate(spectra):
+        cot_spec[index] = spectrum
+    back = backward(
+        [conj_product(codes_spec, spectrum) for spectrum in spectra],
+        turn[...], second_back[...], first_back[...],
+    )
+    for index in range(DP):
+        grad = back[:, index * LANES : (index + 1) * LANES] * scale + direct * cots[index]
+        part = pl.ds(index * SEQ, SEQ)
+        for row in range(ROWS):
+            wide[part, row, :] = grad[row * SEQ : (row + 1) * SEQ]
+        grad_out[part] = wide[part].astype(BF16)
+    for step in everyone[:EARLY]:
+        _, to_place, other = target(step)
+        post(3, grad_out.at[to_place], home_grad.at[place], other)
 
     drain(2, sig_in, ALL - 1).wait_recv()
     wide[...] = sig_in[...].astype(F32)
     total_spec = jnp.zeros((HALF, 2 * LANES), F32)
-    for pair in (0, 2):
-        near = DP_STEPS[pair : pair + 2]
-        which = [cores[step[1]] * 2 + sides[step[0]] for step in near]
-        both = jnp.concatenate([gather(wide, index * SEQ) for index in which], axis=1)
-        spectra = forward(both.astype(BF16), first[...], turn[...], second[...])
-        for index, spectrum in enumerate(spectra):
-            total_spec += conj_product(spectrum, cot_spec[pair + index])
+    spectra = forward(
+        jnp.concatenate([gather(wide, index * SEQ) for index in range(DP)], axis=1).astype(BF16),
+        first[...], turn[...], second[...],
+    )
+    for index, spectrum in enumerate(spectra):
+        total_spec += conj_product(spectrum, cot_spec[index])
     total = backward([total_spec], turn[...], second_back[...], first_back[...])
     total = total * (2.0 / POINTS)
     for row in range(ROWS):
@@ -274,11 +283,32 @@
     for step in hops(((0, 0), (1, 0))):
         if any(step):
             to_seq, _, other = target(step)
-            post(4, total_out.at[to_seq], home_total.at[place], other)
-    home_total[pl.ds(place, 1)] = total_out[pl.ds(s, 1)]
+            post(4, total_out.at[to_seq], home_total.at[s + side * SEQ], other)
+    for step in everyone[EARLY:]:
+        _, to_place, other = target(step)
+        post(3, grad_out.at[to_place], home_grad.at[place], other)
+    home_total[pl.ds(s + side * SEQ, 1)] = total_out[pl.ds(s, 1)]
     home_grad[pl.ds(place, 1)] = grad_out[pl.ds(place, 1)]
 
     eye = same((LANES, LANES))
+    half = 2 * SEQ
+    channels = pl.ds(pl.multiple_of(core * half, LANES), half)
+    factor = jnp.exp2(powers[...].astype(F32))
+    factor = jnp.where(core == 0, factor[:, :half], factor[:, half:])
+    drain(4, home_total, half - 1).wait_recv()
+    wide[pl.ds(0, half)] = home_total[...].astype(F32)
+    for row in range(ROWS):
+        part = pl.ds(row * LANES, LANES)
+        value = dot_nt(eye, wide[pl.ds(0, half), row, :].astype(BF16))
+        filter_grad[part, :] = (mask[part, channels].astype(F32) * factor * value).astype(BF16)
+    across_core = pltpu.make_async_remote_copy(
+        src_ref=filter_grad, dst_ref=filter_hbm.at[core],
+        send_sem=send_sem.at[5], recv_sem=recv_sem.at[5],
+        device_id=me + 1 - 2 * core, device_id_type=LOGICAL,
+    )
+    across_core.start()
+    store_filter = pltpu.make_async_copy(filter_grad, filter_hbm.at[core], store_sem.at[1])
+    store_filter.start()
     drain(3, home_grad, ALL - 1).wait_recv()
     wide[...] = home_grad[...].astype(F32)
     for row in range(ROWS):
@@ -286,63 +316,43 @@
         input_grad[pl.ds(row * LANES, LANES), :] = dot_nt(eye, grad).astype(BF16)
     store_input = pltpu.make_async_copy(input_grad, input_hbm, store_sem.at[0])
     store_input.start()
-
-    half = 2 * SEQ
-    drain(4, home_total, half - 1).wait_recv()
-    mine = home_total.at[pl.ds(core * half, half)]
-    across_core = pltpu.make_async_remote_copy(
-        src_ref=mine, dst_ref=mine, send_sem=send_sem.at[5], recv_sem=recv_sem.at[5],
-        device_id=me + 1 - 2 * core, device_id_type=LOGICAL,
-    )
-    across_core.start()
-    factor = jnp.exp2(powers[...].astype(F32)) * (1.0 / math.sqrt(DP * HALF * LANES))
-
-    def finish(which):
-        channels = pl.ds(pl.multiple_of(which * half, LANES), half)
-        wide[pl.ds(0, half)] = home_total[pl.ds(which * half, half)].astype(F32)
-        chosen = jnp.where(which == 0, factor[:, :half], factor[:, half:])
-        for row in range(ROWS):
-            part = pl.ds(row * LANES, LANES)
-            value = dot_nt(eye, wide[pl.ds(0, half), row, :].astype(BF16))
-            filter_grad[part, channels] = mask[part, channels].astype(F32) * chosen * value
-
-    finish(core)
-    across_core.wait_recv()
-    finish(1 - core)
-    store_filter = pltpu.make_async_copy(filter_grad, filter_hbm, store_sem.at[1])
-    store_filter.start()
     drain(0, codes_out, SEQ - 1).wait_send()
     drain(1, cot_out, ALL - 1).wait_send()
     drain(2, sig_out, ALL - 1).wait_send()
     drain(3, grad_out, ALL - 1).wait_send()
     drain(4, home_total, half - 1).wait_send()
-    across_core.wait_send()
+    store_filter.wait()
+    across_core.wait()
     store_input.wait()
-    store_filter.wait()
-
-
-def last_kernel(input_main, filter_main, input_grad, filter_grad, input_held, filter_held, sem):
-    steps = []
-    for source, held, result in (
-        (filter_main, filter_held, filter_grad), (input_main, input_held, input_grad)
-    ):
-        size = source.shape[0] // 4
-        for index in range(4):
-            part = pl.ds(index * size, size)
-            at = len(steps)
-            steps.append(
-                (
-                    pltpu.make_async_copy(source.at[part], held.at[part], sem.at[0, at]),
-                    pltpu.make_async_copy(held.at[part], result.at[part], sem.at[1, at]),
-                )
-            )
-    for load, _ in steps:
+
+
+def last_kernel(input_main, filter_main, input_grad, filter_grad, input_held, halves, held, load_sem, store_sem):
+    load_halves = [
+        pltpu.make_async_copy(filter_main.at[index], halves.at[index], load_sem.at[index])
+        for index in range(2)
+    ]
+    load_input = pltpu.make_async_copy(input_main, input_held, load_sem.at[2])
+    for load in load_halves:
         load.start()
-    for load, store in steps:
+    load_input.start()
+    for load in load_halves:
         load.wait()
-        store.start()
-    for _, store in steps:
+    stores = []
+    for row in range(ROWS):
+        part = pl.ds(row * LANES, LANES)
+        for index in range(2):
+            value = halves[index, part, :].astype(F32) * (1.0 / math.sqrt(DP * HALF * LANES))
+            held[part, pl.ds(index * LANES, LANES)] = value
+        stores.append(
+            pltpu.make_async_copy(held.at[part], filter_grad.at[part], store_sem.at[row])
+        )
+        stores[-1].start()
+    load_input.wait()
+    store_input = pltpu.make_async_copy(input_held, input_grad, store_sem.at[ROWS])
+    store_input.start()
+    for store in stores:
         store.wait()
+    store_input.wait()
 
 
 def per_device(signal, cotangent, filter_codes, keep_mask, exponents, skip):
@@ -357,7 +367,7 @@
     )
     input_main, filter_main = pl.pallas_call(
         main_kernel,
-        out_shape=results,
+        out_shape=(results[0], jax.ShapeDtypeStruct((2, span, width // 2), BF16)),
         in_specs=[hbm] * 4 + [smem] * 2 + [hbm] * 6,
         out_specs=(hbm, hbm),
         scratch_shapes=[
@@ -377,9 +387,9 @@
             pltpu.VMEM((ALL,) + message, BF16),
             pltpu.VMEM((SEQ,) + message, BF16),
             pltpu.VMEM((ALL,) + message, BF16),
-            pltpu.VMEM((ALL,) + message, BF16),
+            pltpu.VMEM((2 * SEQ,) + message, BF16),
             pltpu.VMEM((span, width), BF16),
-            pltpu.VMEM((span, width), F32),
+            pltpu.VMEM((span, width // 2), BF16),
             pltpu.VMEM((DP, HALF, 2 * LANES), F32),
             pltpu.SemaphoreType.DMA((6,)),
             pltpu.SemaphoreType.DMA((6,)),
@@ -401,8 +411,10 @@
         out_specs=(hbm, hbm),
         scratch_shapes=[
             pltpu.VMEM((span, width), BF16),
+            pltpu.VMEM((2, span, width // 2), BF16),
             pltpu.VMEM((span, width), F32),
-            pltpu.SemaphoreType.DMA((2, 8)),
+            pltpu.SemaphoreType.DMA((3,)),
+            pltpu.SemaphoreType.DMA((ROWS + 1,)),
         ],
         compiler_params=pltpu.CompilerParams(vmem_limit_bytes=VMEM_LIMIT),
         name="last",

time: 46.7 us -> 45.3 us (0.970)
  Pallas kernels: 46 us -> 44.6 us
    pallas_call x1, Pallas kernels: 44 us -> 42.6 us  [per_device(): pl.pallas_call(main_kernel, out_shape=(results[0], jax.ShapeDtypeStruct((...]
where the time goes in v3:
time: 45.3 us; the launch traced here: 45.2 us
  Pallas kernels  44.6 us (98%)
  between operations  0.64 us (1%)
    pallas_call x1, Pallas kernels, per_device(): pl.pallas_call(main_kernel, out_shape=(results[0], jax.ShapeDtypeStruct((...  42.6 us
    pallas_call x1, Pallas kernels, per_device(): pl.pallas_call(last_kernel, out_shape=results, in_specs=[hbm, hbm], out_s...  1.92 us

profile of v3, /device:TPU:1, one launch (start us, length us, event | category | flops | bytes accessed | tf_op | source)
XLA Modules:
  0.0 45.2 jit_solution(604316528432767700)
XLA Ops:
  0.6 42.6 %main.1 = (bf16[512,256]{1,0:T(8,128)(2,1)}, bf16[2,512,128]{2,1,0:T(8,128)(2,1)}) custom-call(bf16[512,256]{1,0:T(8,128)(2,1)} %bitcast.4, bf16[512,256]{1,0:T(8,128)(2,1)} %bitcast.5, bf16[512,256]{1,0:T(8,128)(2,1)} %codes_hbm.1, s32[512,256]{1,0:T(8,128)} %mask_hbm.1, s32[256]{0:T(256)} %exponents.1, f32[256]{0:T(256)} %skip.1, s32[1,256]{1,0:T(1,128)} %bitcast.6, ...), custom_call_target="tpu_custom_call" | custom-call | tf_op jit(solution)/shard_map/main/pallas_call | solution.py:368
  43.3 1.9 %last.1 = (bf16[512,256]{1,0:T(8,128)(2,1)}, f32[512,256]{1,0:T(8,128)}) custom-call(bf16[512,256]{1,0:T(8,128)(2,1)} %get-tuple-element.6.input_main, bf16[2,512,128]{2,1,0:T(8,128)(2,1)} %get-tuple-element.7.filter_main), custom_call_target="tpu_custom_call" | custom-call | tf_op jit(solution)/shard_map/last/pallas_call | solution.py:407

commit v4 on v3

--- a/solution.py
+++ b/solution.py
@@ -145,11 +145,11 @@
 def main_kernel(
     signal_hbm, cotangent_hbm, codes_hbm, mask_hbm, exponents, skip, powers_hbm,
     first_hbm, turn_hbm, second_hbm, second_back_hbm, first_back_hbm,
-    input_hbm, filter_hbm,
+    input_main, filter_main,
     signal, cotangent, codes, mask, powers, first, turn, second, second_back, first_back,
     wide, codes_out, cot_out, sig_out, codes_in, cot_in, sig_in, grad_out, total_out,
-    home_grad, home_total, input_grad, filter_grad,
-    cot_spec, send_sem, recv_sem, load_sem, store_sem,
+    home_grad, home_total,
+    cot_spec, send_sem, recv_sem, load_sem,
 ):
     loads = [
         pltpu.make_async_copy(source, target, load_sem.at[index])
@@ -300,65 +300,46 @@
     for row in range(ROWS):
         part = pl.ds(row * LANES, LANES)
         value = dot_nt(eye, wide[pl.ds(0, half), row, :].astype(BF16))
-        filter_grad[part, :] = (mask[part, channels].astype(F32) * factor * value).astype(BF16)
+        value = mask[part, channels].astype(F32) * factor * value
+        filter_main[core, part, :] = value.astype(BF16)
     across_core = pltpu.make_async_remote_copy(
-        src_ref=filter_grad, dst_ref=filter_hbm.at[core],
+        src_ref=filter_main.at[core], dst_ref=filter_main.at[core],
         send_sem=send_sem.at[5], recv_sem=recv_sem.at[5],
         device_id=me + 1 - 2 * core, device_id_type=LOGICAL,
     )
     across_core.start()
-    store_filter = pltpu.make_async_copy(filter_grad, filter_hbm.at[core], store_sem.at[1])
-    store_filter.start()
     drain(3, home_grad, ALL - 1).wait_recv()
     wide[...] = home_grad[...].astype(F32)
     for row in range(ROWS):
         grad = wide[:, row, :].astype(BF16)
-        input_grad[pl.ds(row * LANES, LANES), :] = dot_nt(eye, grad).astype(BF16)
-    store_input = pltpu.make_async_copy(input_grad, input_hbm, store_sem.at[0])
-    store_input.start()
+        input_main[pl.ds(row * LANES, LANES), :] = dot_nt(eye, grad).astype(BF16)
     drain(0, codes_out, SEQ - 1).wait_send()
     drain(1, cot_out, ALL - 1).wait_send()
     drain(2, sig_out, ALL - 1).wait_send()
     drain(3, grad_out, ALL - 1).wait_send()
     drain(4, home_total, half - 1).wait_send()
-    store_filter.wait()
     across_core.wait()
-    store_input.wait()
-
-
-def last_kernel(input_main, filter_main, input_grad, filter_grad, input_held, halves, held, load_sem, store_sem):
-    load_halves = [
-        pltpu.make_async_copy(filter_main.at[index], halves.at[index], load_sem.at[index])
-        for index in range(2)
-    ]
-    load_input = pltpu.make_async_copy(input_main, input_held, load_sem.at[2])
-    for load in load_halves:
-        load.start()
-    load_input.start()
-    for load in load_halves:
-        load.wait()
-    stores = []
+
+
+def last_kernel(input_main, filter_main, input_grad, filter_grad, held, sem):
+    stores = [pltpu.make_async_copy(input_main, input_grad, sem.at[ROWS])]
+    stores[0].start()
     for row in range(ROWS):
         part = pl.ds(row * LANES, LANES)
         for index in range(2):
-            value = halves[index, part, :].astype(F32) * (1.0 / math.sqrt(DP * HALF * LANES))
+            value = filter_main[index, part, :].astype(F32) * (1.0 / math.sqrt(DP * HALF * LANES))
             held[part, pl.ds(index * LANES, LANES)] = value
-        stores.append(
-            pltpu.make_async_copy(held.at[part], filter_grad.at[part], store_sem.at[row])
-        )
+        stores.append(pltpu.make_async_copy(held.at[part], filter_grad.at[part], sem.at[row]))
         stores[-1].start()
-    load_input.wait()
-    store_input = pltpu.make_async_copy(input_held, input_grad, store_sem.at[ROWS])
-    store_input.start()
     for store in stores:
         store.wait()
-    store_input.wait()
 
 
 def per_device(signal, cotangent, filter_codes, keep_mask, exponents, skip):
     span, width = signal.shape[1], signal.shape[2]
     smem = pl.BlockSpec(memory_space=pltpu.SMEM)
     hbm = pl.BlockSpec(memory_space=pltpu.HBM)
+    vmem = pl.BlockSpec(memory_space=pltpu.VMEM)
     constants = [jnp.asarray(table) for table in tables()]
     message = (ROWS, LANES)
     results = (
@@ -367,9 +348,9 @@
     )
     input_main, filter_main = pl.pallas_call(
         main_kernel,
-        out_shape=(results[0], jax.ShapeDtypeStruct((2, span, width // 2), BF16)),
+        out_shape=(pltpu.VMEM((span, width), BF16), pltpu.VMEM((2, span, width // 2), BF16)),
         in_specs=[hbm] * 4 + [smem] * 2 + [hbm] * 6,
-        out_specs=(hbm, hbm),
+        out_specs=(vmem, vmem),
         scratch_shapes=[
             pltpu.VMEM((span, width), BF16),
             pltpu.VMEM((span, width), BF16),
@@ -388,13 +369,10 @@
             pltpu.VMEM((SEQ,) + message, BF16),
             pltpu.VMEM((ALL,) + message, BF16),
             pltpu.VMEM((2 * SEQ,) + message, BF16),
-            pltpu.VMEM((span, width), BF16),
-            pltpu.VMEM((span, width // 2), BF16),
             pltpu.VMEM((DP, HALF, 2 * LANES), F32),
             pltpu.SemaphoreType.DMA((6,)),
             pltpu.SemaphoreType.DMA((6,)),
             pltpu.SemaphoreType.DMA((10,)),
-            pltpu.SemaphoreType.DMA((2,)),
         ],
         compiler_params=pltpu.CompilerParams(
             collective_id=0, has_side_effects=True, vmem_limit_bytes=VMEM_LIMIT
@@ -407,16 +385,13 @@
     input_grad, filter_grad = pl.pallas_call(
         last_kernel,
         out_shape=results,
-        in_specs=[hbm, hbm],
+        in_specs=[vmem, vmem],
         out_specs=(hbm, hbm),
         scratch_shapes=[
-            pltpu.VMEM((span, width), BF16),
-            pltpu.VMEM((2, span, width // 2), BF16),
             pltpu.VMEM((span, width), F32),
-            pltpu.SemaphoreType.DMA((3,)),
             pltpu.SemaphoreType.DMA((ROWS + 1,)),
         ],
-        compiler_params=pltpu.CompilerParams(vmem_limit_bytes=VMEM_LIMIT),
+        compiler_params=pltpu.CompilerParams(vmem_limit_bytes=4 << 20),
         name="last",
     )(input_main, filter_main)
     return input_grad.reshape(signal.shape), filter_grad

time: 45.3 us -> 44.2 us (0.976)
  Pallas kernels: 44.6 us -> 43.4 us
    pallas_call x2, Pallas kernels: 44.6 us -> 43.4 us  [the longest x1 42.5 us: per_device(): pl.pallas_call(main_kernel, out_shape=(pltpu.VMEM((span, width), BF16), p...]
where the time goes in v4:
time: 44.2 us; the launch traced here: 44.1 us
  Pallas kernels  43.4 us (98%)
  between operations  0.64 us (1%)
    pallas_call x1, Pallas kernels, per_device(): pl.pallas_call(main_kernel, out_shape=(pltpu.VMEM((span, width), BF16), p...  42.5 us
    pallas_call x1, Pallas kernels, per_device(): pl.pallas_call(last_kernel, out_shape=results, in_specs=[vmem, vmem], out...  0.92 us

profile of v4, /device:TPU:1, one launch (start us, length us, event | category | flops | bytes accessed | tf_op | source)
XLA Modules:
  0.0 44.1 jit_solution(2882767387705528214)
XLA Ops:
  0.6 42.5 %main.1 = (bf16[512,256]{1,0:T(8,128)(2,1)S(1)}, bf16[2,512,128]{2,1,0:T(8,128)(2,1)S(1)}) custom-call(bf16[512,256]{1,0:T(8,128)(2,1)} %bitcast.4, bf16[512,256]{1,0:T(8,128)(2,1)} %bitcast.5, bf16[512,256]{1,0:T(8,128)(2,1)} %codes_hbm.1, s32[512,256]{1,0:T(8,128)} %mask_hbm.1, s32[256]{0:T(256)} %exponents.1, f32[256]{0:T(256)} %skip.1, ...), custom_call_target="tpu_custom_call" | custom-call | tf_op jit(solution)/shard_map/main/pallas_call | solution.py:349
  43.1 0.9 %last.1 = (bf16[512,256]{1,0:T(8,128)(2,1)}, f32[512,256]{1,0:T(8,128)}) custom-call(bf16[512,256]{1,0:T(8,128)(2,1)S(1)} %get-tuple-element.6.input_main, bf16[2,512,128]{2,1,0:T(8,128)(2,1)S(1)} %get-tuple-element.7.filter_main), custom_call_target="tpu_custom_call" | custom-call | tf_op jit(solution)/shard_map/last/pallas_call | solution.py:385

commit v5 on v4

--- a/solution.py
+++ b/solution.py
@@ -115,11 +115,11 @@
 DP_STEPS = ((1, 1), (1, 0), (0, 1), (0, 0))
 
 
-def hops(near):
+def hops(near, weight):
     def distance(step):
         up, across, along, side, _ = step
         turns = min(across, X - across) + ((0, 1), (2, 1))[up][side]
-        return 2 * turns + min(along, Z - along)
+        return weight * turns + min(along, Z - along)
 
     steps = [
         (up, across, along, side, core)
@@ -191,9 +191,9 @@
         to_seq = seq_at[seq_step]
         return to_seq, place_at[near] + to_seq, first_at[seq_step] + dp_at[near][1]
 
-    everyone = [step for step in hops(DP_STEPS) if any(step)]
+    everyone = [step for step in hops(DP_STEPS, 1.5) if any(step)]
     barrier = pltpu.get_barrier_semaphore()
-    for step in everyone:
+    for step in hops(DP_STEPS, 1)[: ALL - 1]:
         pl.semaphore_signal(barrier, inc=1, device_id=target(step)[2], device_id_type=LOGICAL)
 
     def post(index, source, destination, other):
@@ -218,7 +218,7 @@
     cot_out[...] = spread(wide, dot_nt(eye, cotangent[...]), ALL)
     pl.semaphore_wait(barrier, ALL - 1)
 
-    for step in hops(((0, 0),)):
+    for step in hops(((0, 0),), 1.5):
         if any(step):
             to_seq, _, other = target(step)
             post(0, codes_out.at[to_seq], codes_in.at[s], other)
@@ -280,7 +280,7 @@
     for row in range(ROWS):
         wide[pl.ds(0, SEQ), row, :] = total[row * SEQ : (row + 1) * SEQ]
     total_out[...] = wide[pl.ds(0, SEQ)].astype(BF16)
-    for step in hops(((0, 0), (1, 0))):
+    for step in hops(((0, 0), (1, 0)), 1.5):
         if any(step):
             to_seq, _, other = target(step)
             post(4, total_out.at[to_seq], home_total.at[s + side * SEQ], other)
@@ -290,7 +290,6 @@
     home_total[pl.ds(s + side * SEQ, 1)] = total_out[pl.ds(s, 1)]
     home_grad[pl.ds(place, 1)] = grad_out[pl.ds(place, 1)]
 
-    eye = same((LANES, LANES))
     half = 2 * SEQ
     channels = pl.ds(pl.multiple_of(core * half, LANES), half)
     factor = jnp.exp2(powers[...].astype(F32))
@@ -299,7 +298,7 @@
     wide[pl.ds(0, half)] = home_total[...].astype(F32)
     for row in range(ROWS):
         part = pl.ds(row * LANES, LANES)
-        value = dot_nt(eye, wide[pl.ds(0, half), row, :].astype(BF16))
+        value = wide[pl.ds(0, half), row, :].T
         value = mask[part, channels].astype(F32) * factor * value
         filter_main[core, part, :] = value.astype(BF16)
     across_core = pltpu.make_async_remote_copy(
@@ -311,8 +310,7 @@
     drain(3, home_grad, ALL - 1).wait_recv()
     wide[...] = home_grad[...].astype(F32)
     for row in range(ROWS):
-        grad = wide[:, row, :].astype(BF16)
-        input_main[pl.ds(row * LANES, LANES), :] = dot_nt(eye, grad).astype(BF16)
+        input_main[pl.ds(row * LANES, LANES), :] = wide[:, row, :].T.astype(BF16)
     drain(0, codes_out, SEQ - 1).wait_send()
     drain(1, cot_out, ALL - 1).wait_send()
     drain(2, sig_out, ALL - 1).wait_send()

time: 44.2 us -> 44.1 us (level)
  no operation moved by 1% of the time
where the time goes in v5:
time: 44.1 us; the launch traced here: 44 us
  Pallas kernels  43.3 us (98%)
  between operations  0.64 us (1%)
    pallas_call x1, Pallas kernels, per_device(): pl.pallas_call(main_kernel, out_shape=(pltpu.VMEM((span, width), BF16), p...  42.4 us
    pallas_call x1, Pallas kernels, per_device(): pl.pallas_call(last_kernel, out_shape=results, in_specs=[vmem, vmem], out...  0.92 us

profile of v5, /device:TPU:1, one launch (start us, length us, event | category | flops | bytes accessed | tf_op | source)
XLA Modules:
  0.0 44.0 jit_solution(8713373995735746498)
XLA Ops:
  0.6 42.4 %main.1 = (bf16[512,256]{1,0:T(8,128)(2,1)S(1)}, bf16[2,512,128]{2,1,0:T(8,128)(2,1)S(1)}) custom-call(bf16[512,256]{1,0:T(8,128)(2,1)} %bitcast.4, bf16[512,256]{1,0:T(8,128)(2,1)} %bitcast.5, bf16[512,256]{1,0:T(8,128)(2,1)} %codes_hbm.1, s32[512,256]{1,0:T(8,128)} %mask_hbm.1, s32[256]{0:T(256)} %exponents.1, f32[256]{0:T(256)} %skip.1, ...), custom_call_target="tpu_custom_call" | custom-call | tf_op jit(solution)/shard_map/main/pallas_call | solution.py:347
  43.0 0.9 %last.1 = (bf16[512,256]{1,0:T(8,128)(2,1)}, f32[512,256]{1,0:T(8,128)}) custom-call(bf16[512,256]{1,0:T(8,128)(2,1)S(1)} %get-tuple-element.6.input_main, bf16[2,512,128]{2,1,0:T(8,128)(2,1)S(1)} %get-tuple-element.7.filter_main), custom_call_target="tpu_custom_call" | custom-call | tf_op jit(solution)/shard_map/last/pallas_call | solution.py:383

commit v6 on v5

--- a/solution.py
+++ b/solution.py
@@ -96,6 +96,10 @@
             jnp.concatenate([real * cos + imag * sin, imag * cos - real * sin], axis=0)
         )
     high, low = split(jnp.concatenate(columns, axis=1))
+    if len(spectra) == 1:
+        both = dot(first_back[:, : 2 * HALF], jnp.concatenate([high, low], axis=1))
+        rest = dot(first_back[:, 2 * HALF : 4 * HALF], high)
+        return both[:, :LANES] + both[:, LANES:] + rest
     return dot(first_back, jnp.concatenate([high, high, low], axis=0))
 
 
@@ -136,6 +140,12 @@
     for row in range(ROWS):
         wide[pl.ds(0, count), row, :] = values[:, row * LANES : (row + 1) * LANES]
     return wide[pl.ds(0, count)].astype(BF16)
+
+
+def turn_rows(wide, array):
+    for row in range(ROWS):
+        wide[:, row, :] = array[pl.ds(row * LANES, LANES), :].astype(F32).T
+    return wide[...].astype(BF16)
 
 
 def gather(wide, start):
@@ -214,8 +224,7 @@
     loads[0].wait()
     codes_out[...] = spread(wide, dot_nt(same((SEQ, ALL), q * SEQ), codes[...]), SEQ)
     loads[1].wait()
-    eye = same((ALL, ALL))
-    cot_out[...] = spread(wide, dot_nt(eye, cotangent[...]), ALL)
+    cot_out[...] = turn_rows(wide, cotangent)
     pl.semaphore_wait(barrier, ALL - 1)
 
     for step in hops(((0, 0),), 1.5):
@@ -227,7 +236,7 @@
         post(1, cot_out.at[to_place], cot_in.at[place], other)
 
     loads[2].wait()
-    sig_out[...] = spread(wide, dot_nt(eye, signal[...]), ALL)
+    sig_out[...] = turn_rows(wide, signal)
     for step in everyone:
         _, to_place, other = target(step)
         post(2, sig_out.at[to_place], sig_in.at[place], other)

time: 44.1 us -> 44 us (level)
  no operation moved by 1% of the time
where the time goes in v6:
time: 44 us; the launch traced here: 43.9 us
  Pallas kernels  43.2 us (98%)
  between operations  0.64 us (1%)
    pallas_call x1, Pallas kernels, per_device(): pl.pallas_call(main_kernel, out_shape=(pltpu.VMEM((span, width), BF16), p...  42.3 us
    pallas_call x1, Pallas kernels, per_device(): pl.pallas_call(last_kernel, out_shape=results, in_specs=[vmem, vmem], out...  0.92 us

profile of v6, /device:TPU:1, one launch (start us, length us, event | category | flops | bytes accessed | tf_op | source)
XLA Modules:
  0.0 43.9 jit_solution(5724729690881181544)
XLA Ops:
  0.6 42.3 %main.1 = (bf16[512,256]{1,0:T(8,128)(2,1)S(1)}, bf16[2,512,128]{2,1,0:T(8,128)(2,1)S(1)}) custom-call(bf16[512,256]{1,0:T(8,128)(2,1)} %bitcast.4, bf16[512,256]{1,0:T(8,128)(2,1)} %bitcast.5, bf16[512,256]{1,0:T(8,128)(2,1)} %codes_hbm.1, s32[512,256]{1,0:T(8,128)} %mask_hbm.1, s32[256]{0:T(256)} %exponents.1, f32[256]{0:T(256)} %skip.1, ...), custom_call_target="tpu_custom_call" | custom-call | tf_op jit(solution)/shard_map/main/pallas_call | solution.py:356
  43.0 0.9 %last.1 = (bf16[512,256]{1,0:T(8,128)(2,1)}, f32[512,256]{1,0:T(8,128)}) custom-call(bf16[512,256]{1,0:T(8,128)(2,1)S(1)} %get-tuple-element.6.input_main, bf16[2,512,128]{2,1,0:T(8,128)(2,1)S(1)} %get-tuple-element.7.filter_main), custom_call_target="tpu_custom_call" | custom-call | tf_op jit(solution)/shard_map/last/pallas_call | solution.py:392
